TPU v7x, 32 devices: a whole 2x2x4 slice. The times are simulated.
32 devices in a mesh: grp: 4 (over z), dev: 8 (over y, x, core).
Axes of the slice: x: 2, y: 2, z: 4, core: 2. Of those that a mesh axis runs over, the one named last changes fastest.
Arguments:
- amplitudes: bfloat16 [1024, 589824], P('dev', 'grp'), may hold values from -6 to 6
- singles: float32 [32, 768], replicated, may hold values from -5 to 5
- pair_source: int32 [1024], replicated, may hold values from 0 to 1023, each once
- integrals: bfloat16 [589824, 512], P(('grp', 'dev')), may hold values from -0.0078125 to 0.0078125
Outputs:
- ladder: float32 [1024, 512], P('dev')
Inputs may be any that keep to these rules, and one draw needn't show every extreme that they name: `pair_source`: each occupied pair appears exactly once.
All inputs are finite; a program needn't handle non-finite values.
Results may differ from a plain program's by a relative error of at most 0.0029.
Values may be sent and summed in bfloat16 or wider, within the bound.
A program may use at most 320 MiB of HBM per device.

v0:
```python
import jax
import jax.numpy as jnp
from jax import lax
from jax.sharding import PartitionSpec as P


def body(amplitudes, singles, pair_source, integrals):
    local = lax.all_to_all(amplitudes, "dev", split_axis=1, concat_axis=0, tiled=True)
    occupied = singles.shape[0]
    virtual = singles.shape[1]
    count = local.shape[1]
    first = (lax.axis_index("grp") * lax.axis_size("dev") + lax.axis_index("dev")) * count
    cd_index = first + jnp.arange(count, dtype=jnp.int32)
    c_part = cd_index // virtual
    d_part = cd_index % virtual
    labels = jnp.arange(virtual, dtype=jnp.int32)[:, None]
    pick_c = (labels == c_part[None, :]).astype(jnp.float32)
    pick_d = (labels == d_part[None, :]).astype(jnp.float32)
    left_factor = jnp.dot(
        singles, pick_c, precision=lax.Precision.HIGHEST, preferred_element_type=jnp.float32
    )
    right_factor = jnp.dot(
        singles, pick_d, precision=lax.Precision.HIGHEST, preferred_element_type=jnp.float32
    )
    dressing = (left_factor[:, None, :] * right_factor[None, :, :]).reshape(
        occupied * occupied, count
    )
    ordered = jnp.take(local, pair_source, axis=0)
    tau = (ordered.astype(jnp.float32) + dressing).astype(jnp.bfloat16)
    share = occupied * occupied // lax.axis_size("dev")
    partial_value = jnp.dot(tau, integrals, preferred_element_type=jnp.float32)
    summed = lax.psum(partial_value, ("grp", "dev"))
    return lax.dynamic_slice_in_dim(summed, lax.axis_index("dev") * share, share, 0)


def solution(mesh):
    placed = (P("dev", "grp"), P(), P(), P(("grp", "dev"), None))
    return jax.shard_map(
        body, mesh=mesh, in_specs=placed, out_specs=P("dev", None), check_vma=False
    )
```

profile of v0, /device:TPU:0, one launch (start us, length us, event | category | flops | bytes accessed | tf_op | source)
XLA Modules:
  0.0 772.0 jit_solution(15173130806688675399)
XLA Ops:
  6.5 0.0 copy-start
  6.5 25.5 %copy.8 = bf16[16,8,8,18432]{3,2,0,1:T(8,128)(2,1)} copy(bf16[16,8,8,18432]{3,2,1,0:T(8,128)(2,1)} %bitcast.20) | data formatting | bytes 75497472 | tf_op jit(solution)/shard_map/all_to_all | solution.py:8
  32.0 0.0 copy-start.2
  32.0 7.7 all-to-all-start
  39.7 0.0 all-reduce.2.cloned.1.call-start
  39.8 0.0 copy-done.2
  39.8 0.1 add_select_fusion
  39.9 0.0 copy-done
  39.9 20.2 %fusion.5 = f32[32,18432]{1,0:T(8,128)S(1)} fusion(f32[32,768]{1,0:T(8,128)S(1)} %copy-done, s32[18432]{0:T(1024)S(1)} %get-tuple-element.5), kind=kOutput, calls=%fused_computation.11 | convolution fusion | flops 5449973760 | bytes 2531328 | tf_op jit(solution)/shard_map/dot_general | solution.py:22
  60.1 21.7 %fusion.6 = f32[32,18432]{1,0:T(8,128)} fusion(f32[32,768]{1,0:T(8,128)S(1)} %copy-done, s32[18432]{0:T(1024)S(1)} %get-tuple-element.6), kind=kOutput, calls=%fused_computation.12 | convolution fusion | flops 5449973760 | bytes 2531328 | tf_op jit(solution)/shard_map/dot_general | solution.py:19
  81.8 25.2 %broadcast_multiply_fusion = f32[32,32,18432]{2,1,0:T(8,128)} fusion(f32[32,18432]{1,0:T(8,128)S(1)} %fusion.5, f32[32,18432]{1,0:T(8,128)} %fusion.6), kind=kLoop, calls=%fused_computation.8 | loop fusion | flops 18874368 | bytes 80216064 | tf_op jit(solution)/shard_map/mul | solution.py:25
  107.0 341.9 %all-to-all-done = bf16[128,8,18432]{2,0,1:T(8,128)(2,1)} async-done(((bf16[128,8,18432]{2,0,1:T(8,128)(2,1)}), bf16[128,8,18432]{2,0,1:T(8,128)(2,1)}, u32[]{:S(2)}, u32[]{:S(2)}) %all-to-all-start) | async-done | bytes 37748768 | tf_op jit(solution)/shard_map/all_to_all | solution.py:8
  448.9 104.1 %gather_fusion = bf16[1024,18432]{1,0:T(8,128)(2,1)} fusion(bf16[1024,18432]{1,0:T(8,128)(2,1)} %bitcast.1, s32[1024]{0:T(1024)S(1)} %fusion.12), kind=kCustom, calls=%fused_computation | custom fusion | bytes 75501568 | tf_op jit(solution)/shard_map/jit(_take)/gather | solution.py:28
  553.0 0.0 copy-start.1
  553.0 47.7 %fusion = bf16[1024,18432]{1,0:T(8,128)(2,1)} fusion(f32[32,32,18432]{2,1,0:T(8,128)} %broadcast_multiply_fusion, bf16[1024,18432]{1,0:T(8,128)(2,1)} %gather_fusion, pred[1024]{0:T(1024)(128)(4,1)S(1)} %compare_and_fusion), kind=kLoop, calls=%fused_computation.2 | loop fusion | flops 75497472 | bytes 150995968 | tf_op jit(solution)/shard_map/convert_element_type | solution.py:29
  600.7 28.1 %fusion.13 = f32[1024,512]{1,0:T(8,128)} fusion(bf16[1024,18432]{1,0:T(8,128)(2,1)} %fusion, bf16[18432,512]{1,0:T(8,128)(2,1)} %param.7), kind=kOutput, calls=%fused_computation.26 | convolution fusion | flops 19327352832 | bytes 58720256 | tf_op jit(solution)/shard_map/dot_general | solution.py:31
  628.8 0.0 all-reduce.2.cloned.1.call-update
  628.8 134.3 %all-reduce.2.cloned.1.call-done = f32[1024,512]{1,0:T(8,128)} async-done(((f32[1024,512]{1,0:T(8,128)}), f32[1024,512]{1,0:T(8,128)}) %all-reduce.2.cloned.1.call-update) | async-done | bytes 2097168 | tf_op jit(solution)/shard_map/psum | solution.py:32
  763.0 1.7 constant_dynamic-slice_fusion
  764.7 0.0 copy-done.1
  (2 shorter events, 0.0 us)
Async XLA Ops:
  6.5 33.3 %copy-start = (f32[32,768]{1,0:T(8,128)S(1)}, f32[32,768]{1,0:T(8,128)}, u32[]{:S(2)}) copy-start(f32[32,768]{1,0:T(8,128)} %param.5) | copy-start | bytes 294916
  32.0 7.7 %copy-start.2 = (s32[1024]{0:T(1024)S(1)}, s32[1024]{0:T(1024)}, u32[]{:S(2)}) copy-start(s32[1024]{0:T(1024)} %param.6) | copy-start | bytes 12292
  32.0 416.9 %all-to-all-start = ((bf16[128,8,18432]{2,0,1:T(8,128)(2,1)}), bf16[128,8,18432]{2,0,1:T(8,128)(2,1)}, u32[]{:S(2)}, u32[]{:S(2)}) async-start(bf16[128,8,18432]{2,0,1:T(8,128)(2,1)} %bitcast.19), calls=%async_computation | async-start | bytes 75497472 | tf_op jit(solution)/shard_map/all_to_all | solution.py:8
  39.7 723.3 %all-reduce.2.cloned.1.call-start = ((), (), s32[]{:S(2)}) async-start(), calls=%async_computation.1 | async-start | bytes 4194304 | tf_op jit(solution)/shard_map/psum | solution.py:32
  553.0 211.7 %copy-start.1 = (f32[32,768]{1,0:T(8,128)S(1)}, f32[32,768]{1,0:T(8,128)}, u32[]{:S(2)}) copy-start(f32[32,768]{1,0:T(8,128)} %param.5) | copy-start | bytes 294916
Sparse Core Ops, SparseCore 0:
  628.9 134.0 all-reduce.1
where the time goes:
time: 781 us; the launch traced here: 772 us
  waiting for transfers between devices  476 us (61%)
  local copies, waits for them, and re-layouts  131 us (17%)
  other arithmetic  73 us (9%)
  matrix products  70 us (9%)
  between operations  13.9 us (2%)
    all_to_all x1, waiting for transfers between devices, body(): lax.all_to_all(amplitudes, 'dev', split_axis=1, concat_axis=0, tiled=True)  342 us
    psum x1, waiting for transfers between devices, body(): summed = lax.psum(partial_value, ('grp', 'dev'))  134 us
    gather x1, local copies, waits for them, and re-layouts, body(): ordered = jnp.take(local, pair_source, axis=0)  104 us
    convert_element_type x1, other arithmetic, body(): tau = (ordered.astype(jnp.float32) + dressing).astype(jnp.bfloat16)  47.7 us
    dot_general x1, matrix products, body(): partial_value = jnp.dot(tau, integrals, preferred_element_type=jnp.float32)  28.1 us
    all_to_all x1, local copies, waits for them, and re-layouts, body(): lax.all_to_all(amplitudes, 'dev', split_axis=1, concat_axis=0, tiled=True)  25.5 us
    mul x1, other arithmetic, body(): left_factor[:, None, :] * right_factor[None, :, :]  25.2 us
    dot_general x1, matrix products, body(): jnp.dot(singles, pick_c, precision=lax.Precision.HIGHEST, preferred_eleme...  21.7 us
  transfers between devices with their start and end apart: 2, of which 2 were waited for; matrix products, arithmetic and copies ran while one was open for 9% of the time, Pallas kernels for 0%

commit v1 on v0

--- a/solution.py
+++ b/solution.py
@@ -29,7 +29,8 @@
     tau = (ordered.astype(jnp.float32) + dressing).astype(jnp.bfloat16)
     share = occupied * occupied // lax.axis_size("dev")
     partial_value = jnp.dot(tau, integrals, preferred_element_type=jnp.float32)
-    summed = lax.psum(partial_value, ("grp", "dev"))
+    front = lax.all_gather(partial_value, ("grp", "dev"))
+    summed = jnp.sum(front, axis=0)
     return lax.dynamic_slice_in_dim(summed, lax.axis_index("dev") * share, share, 0)
 
 

time: 781 us -> 1020 us (1.31)
  waiting for transfers between devices: 476 us -> 699 us
  other arithmetic: 73 us -> 93.9 us
    all_gather x0 -> x1, waiting for transfers between devices: none -> 357 us  [body(): front = lax.all_gather(partial_value, ('grp', 'dev'))]
    psum x1 -> x0, waiting for transfers between devices: 134 us -> none  [body(): summed = lax.psum(partial_value, ('grp', 'dev'))]
    reduce_sum x0 -> x1, other arithmetic: none -> 20.9 us  [body(): summed = jnp.sum(front, axis=0)]
  transfers between devices with their start and end apart: 2 -> 2, of which waited for: 2 -> 2; matrix products, arithmetic and copies ran while one was open for 9% -> 7% of each run, Pallas kernels for 0% -> 0%
where the time goes in v1:
time: 1020 us; the launch traced here: 1010 us
  waiting for transfers between devices  699 us (69%)
  local copies, waits for them, and re-layouts  130 us (13%)
  other arithmetic  93.9 us (9%)
  matrix products  69.9 us (7%)
  between operations  13.9 us (1%)
    all_gather x1, waiting for transfers between devices, body(): front = lax.all_gather(partial_value, ('grp', 'dev'))  357 us
    all_to_all x1, waiting for transfers between devices, body(): lax.all_to_all(amplitudes, 'dev', split_axis=1, concat_axis=0, tiled=True)  342 us
    gather x1, local copies, waits for them, and re-layouts, body(): ordered = jnp.take(local, pair_source, axis=0)  104 us
    convert_element_type x1, other arithmetic, body(): tau = (ordered.astype(jnp.float32) + dressing).astype(jnp.bfloat16)  47.7 us
    dot_general x1, matrix products, body(): partial_value = jnp.dot(tau, integrals, preferred_element_type=jnp.float32)  28 us
    all_to_all x1, local copies, waits for them, and re-layouts, body(): lax.all_to_all(amplitudes, 'dev', split_axis=1, concat_axis=0, tiled=True)  25.5 us
    mul x1, other arithmetic, body(): left_factor[:, None, :] * right_factor[None, :, :]  25.2 us
    dot_general x1, matrix products, body(): jnp.dot(singles, pick_c, precision=lax.Precision.HIGHEST, preferred_eleme...  21.7 us
  transfers between devices with their start and end apart: 2, of which 2 were waited for; matrix products, arithmetic and copies ran while one was open for 7% of the time, Pallas kernels for 0%

profile of v1, /device:TPU:0, one launch (start us, length us, event | category | flops | bytes accessed | tf_op | source)
XLA Modules:
  0.0 1014.4 jit_solution(2865754621683897523)
XLA Ops:
  6.5 0.0 copy-start
  6.5 25.5 %copy.8 = bf16[16,8,8,18432]{3,2,0,1:T(8,128)(2,1)} copy(bf16[16,8,8,18432]{3,2,1,0:T(8,128)(2,1)} %bitcast.21) | data formatting | bytes 75497472 | tf_op jit(solution)/shard_map/all_to_all | solution.py:8
  32.0 0.0 copy-start.2
  32.0 7.7 all-to-all-start
  39.7 0.0 all-gather.3.cloned.1.call-start
  39.8 0.0 copy-done.2
  39.8 0.1 add_select_fusion
  39.9 0.0 copy-done
  39.9 20.2 %fusion.5 = f32[32,18432]{1,0:T(8,128)S(1)} fusion(f32[32,768]{1,0:T(8,128)S(1)} %copy-done, s32[18432]{0:T(1024)S(1)} %get-tuple-element.5), kind=kOutput, calls=%fused_computation.11 | convolution fusion | flops 5449973760 | bytes 2531328 | tf_op jit(solution)/shard_map/dot_general | solution.py:22
  60.1 21.7 %fusion.6 = f32[32,18432]{1,0:T(8,128)} fusion(f32[32,768]{1,0:T(8,128)S(1)} %copy-done, s32[18432]{0:T(1024)S(1)} %get-tuple-element.6), kind=kOutput, calls=%fused_computation.12 | convolution fusion | flops 5449973760 | bytes 2531328 | tf_op jit(solution)/shard_map/dot_general | solution.py:19
  81.8 25.2 %broadcast_multiply_fusion = f32[32,32,18432]{2,1,0:T(8,128)} fusion(f32[32,18432]{1,0:T(8,128)S(1)} %fusion.5, f32[32,18432]{1,0:T(8,128)} %fusion.6), kind=kLoop, calls=%fused_computation.8 | loop fusion | flops 18874368 | bytes 80216064 | tf_op jit(solution)/shard_map/mul | solution.py:25
  107.0 341.9 %all-to-all-done = bf16[128,8,18432]{2,0,1:T(8,128)(2,1)} async-done(((bf16[128,8,18432]{2,0,1:T(8,128)(2,1)}), bf16[128,8,18432]{2,0,1:T(8,128)(2,1)}, u32[]{:S(2)}, u32[]{:S(2)}) %all-to-all-start) | async-done | bytes 37748768 | tf_op jit(solution)/shard_map/all_to_all | solution.py:8
  448.9 104.1 %gather_fusion = bf16[1024,18432]{1,0:T(8,128)(2,1)} fusion(bf16[1024,18432]{1,0:T(8,128)(2,1)} %bitcast.1, s32[1024]{0:T(1024)S(1)} %fusion.12), kind=kCustom, calls=%fused_computation | custom fusion | bytes 75501568 | tf_op jit(solution)/shard_map/jit(_take)/gather | solution.py:28
  553.0 47.7 %fusion = bf16[1024,18432]{1,0:T(8,128)(2,1)} fusion(f32[32,32,18432]{2,1,0:T(8,128)} %broadcast_multiply_fusion, bf16[1024,18432]{1,0:T(8,128)(2,1)} %gather_fusion, pred[1024]{0:T(1024)(128)(4,1)S(1)} %compare_and_fusion), kind=kLoop, calls=%fused_computation.2 | loop fusion | flops 75497472 | bytes 150995968 | tf_op jit(solution)/shard_map/convert_element_type | solution.py:29
  600.6 0.0 copy-start.1
  600.7 28.0 %fusion.13 = f32[1024,512]{1,0:T(8,128)} fusion(bf16[1024,18432]{1,0:T(8,128)(2,1)} %fusion, bf16[18432,512]{1,0:T(8,128)(2,1)} %param.7), kind=kOutput, calls=%fused_computation.26 | convolution fusion | flops 19327352832 | bytes 58720256 | tf_op jit(solution)/shard_map/dot_general | solution.py:31
  628.7 0.0 all-gather.3.cloned.1.call-update
  628.7 356.7 %all-gather.3.cloned.1.call-done = f32[32768,512]{1,0:T(8,128)} async-done(((f32[1024,512]{1,0:T(8,128)}), f32[32768,512]{1,0:T(8,128)}) %all-gather.3.cloned.1.call-update) | async-done | bytes 67108880 | tf_op jit(solution)/shard_map/all_gather | solution.py:32
  985.4 20.9 %reduce_sum.9 = f32[1024,512]{1,0:T(8,128)S(1)} reduce(f32[32,1024,512]{2,1,0:T(8,128)} %bitcast.5, f32[]{:T(128)} %constant.51.clone.1), dimensions={0}, to_apply=%region_0.1 | reduce | flops 16252928 | bytes 69206016 | tf_op jit(solution)/shard_map/reduce_sum | solution.py:33
  1006.3 0.7 constant_dynamic-slice_fusion
  1007.1 0.0 copy-done.1
  (2 shorter events, 0.0 us)
Async XLA Ops:
  6.5 33.3 %copy-start = (f32[32,768]{1,0:T(8,128)S(1)}, f32[32,768]{1,0:T(8,128)}, u32[]{:S(2)}) copy-start(f32[32,768]{1,0:T(8,128)} %param.5) | copy-start | bytes 294916
  32.0 7.7 copy-start.2
  32.0 416.9 %all-to-all-start = ((bf16[128,8,18432]{2,0,1:T(8,128)(2,1)}), bf16[128,8,18432]{2,0,1:T(8,128)(2,1)}, u32[]{:S(2)}, u32[]{:S(2)}) async-start(bf16[128,8,18432]{2,0,1:T(8,128)(2,1)} %bitcast.20), calls=%async_computation | async-start | bytes 75497472 | tf_op jit(solution)/shard_map/all_to_all | solution.py:8
  39.7 945.7 %all-gather.3.cloned.1.call-start = ((), (), s32[]{:S(2)}) async-start(), calls=%async_computation.1 | async-start | bytes 69206016 | tf_op jit(solution)/shard_map/all_gather | solution.py:32
  600.6 406.4 %copy-start.1 = (f32[32,768]{1,0:T(8,128)S(1)}, f32[32,768]{1,0:T(8,128)}, u32[]{:S(2)}) copy-start(f32[32,768]{1,0:T(8,128)} %param.5) | copy-start | bytes 294916
Sparse Core Ops, SparseCore 0:
  628.8 356.5 all-gather.2
